TPU v7x, 32 devices: a whole 2x2x4 slice. The times are simulated.
32 devices in a mesh: seq: 16 (over z, y, core), tp: 2 (over x).
Axes of the slice: x: 2, y: 2, z: 4, core: 2. Of those that a mesh axis runs over, the one named last changes fastest.
Arguments:
- cache: bfloat16 [2, 16, 512, 3072], P(None, 'seq', 'tp'), may hold values from -24 to 24
- cache_len: int32 [16], replicated, may hold values from 1 to 512, 4096 in all
- group: bfloat16 [3, 16, 256, 3072], P(None, 'seq', None, 'tp'), may hold values from -24 to 24
- group_req: int32 [16], replicated, may hold values from 0 to 15, each once
- req_order: int32 [16], replicated, may hold values from 0 to 15, each once
Outputs:
- context: bfloat16 [16, 256, 3072], P('seq', None, 'tp')
Inputs may be any that keep to these rules, and one draw needn't show every extreme that they name: `group_req`: each request once. `req_order`: each request once.
All inputs are finite; a program needn't handle non-finite values.
Results may differ from a plain program's by a relative error of at most 0.0042.
Values may be sent and summed in bfloat16 or wider, within the bound.
A program may use at most 64 MiB of HBM per device.

v0:
```python
import math

import jax
import jax.numpy as jnp
from jax import lax
from jax.sharding import PartitionSpec as P

HD = 96


def inverse_table(permutation):
    numbers = jnp.arange(permutation.shape[0], dtype=jnp.int32)
    matches = permutation[None, :] == numbers[:, None]
    return jnp.sum(jnp.where(matches, numbers[None, :], 0), axis=1)


def online_part(queries, key_rows, value_rows, keep_rows, block_rows, block_count, factor):
    row_count = queries.shape[0]
    head_count = queries.shape[1]

    def add_block(block_index, carry):
        row_top, weight_sum, weighted = carry
        block_start = block_index * block_rows
        scores = (
            jnp.einsum("qhd,khd->hqk", queries, key_rows, preferred_element_type=jnp.float32)
            * factor
        )
        scores = jnp.where(keep_rows(block_start)[None], scores, -jnp.inf)
        new_top = jnp.maximum(row_top, jnp.max(scores, axis=-1))
        rescale = jnp.exp(row_top - new_top)
        weights = jnp.exp(scores - new_top[..., None]).astype(jnp.bfloat16)
        weight_sum = weight_sum * rescale + jnp.sum(weights, axis=-1, dtype=jnp.float32)
        weighted = weighted * rescale[..., None] + jnp.einsum(
            "hqk,khd->hqd", weights, value_rows, preferred_element_type=jnp.float32
        )
        return (new_top, weight_sum, weighted)

    start_top = jnp.full((head_count, row_count), -jnp.inf, jnp.float32)
    start_sum = jnp.zeros((head_count, row_count), jnp.float32)
    start_mixed = jnp.zeros((head_count, row_count, queries.shape[2]), jnp.float32)
    return lax.fori_loop(0, block_count, add_block, (start_top, start_sum, start_mixed))


def combine_parts(first_part, second_part):
    top_one, sum_one, mixed_one = first_part
    top_two, sum_two, mixed_two = second_part
    row_top = jnp.maximum(top_one, top_two)
    factor_one = jnp.exp(top_one - row_top)
    factor_two = jnp.exp(top_two - row_top)
    result = (factor_one[..., None] * mixed_one + factor_two[..., None] * mixed_two) / (
        factor_one * sum_one + factor_two * sum_two
    )[..., None]
    result = jnp.transpose(result, (1, 0, 2))
    return result.reshape(result.shape[0], -1).astype(jnp.bfloat16)


def shards(cache, cache_len, group, group_req, req_order):
    factor = 1.0 / math.sqrt(HD)
    slot_of = inverse_table(req_order)
    source_slot = jnp.take(slot_of, group_req)
    my_request = jnp.take(group_req, lax.axis_index("seq"))
    length = jnp.take(cache_len, my_request)
    row_count = group.shape[2]
    head_count = group.shape[3] // HD
    queries = group[0, 0].reshape(row_count, head_count, HD)
    new_keys = group[1, 0].reshape(row_count, head_count, HD)
    new_values = group[2, 0].reshape(row_count, head_count, HD)
    group_block = min(512, row_count)

    def causal_rows(block_start):
        key_index = block_start + jnp.arange(group_block, dtype=jnp.int32)
        return jnp.arange(row_count, dtype=jnp.int32)[:, None] >= key_index[None, :]

    group_part = online_part(
        queries, new_keys, new_values, causal_rows, group_block, row_count // group_block, factor
    )
    spread = lax.all_to_all(cache, "seq", split_axis=2, concat_axis=1, tiled=True)
    ordered = jnp.take(spread, source_slot, axis=1)
    moved = lax.all_to_all(
        lax.all_to_all(ordered, "seq", split_axis=1, concat_axis=2, tiled=True),
        "tp",
        split_axis=3,
        concat_axis=2,
        tiled=True,
    )
    position_count = moved.shape[2]
    old_keys = moved[0, 0].reshape(position_count, head_count, HD)
    old_values = moved[1, 0].reshape(position_count, head_count, HD)
    cache_block = min(512, position_count)

    def live_rows(block_start):
        positions = block_start + jnp.arange(cache_block, dtype=jnp.int32)
        return (positions < length)[None, :]

    block_total = position_count // cache_block
    cache_part = online_part(
        queries, old_keys, old_values, live_rows, cache_block, block_total, factor
    )
    context = combine_parts(cache_part, group_part)
    return context[None]


def solution(mesh):
    in_specs = (P(None, "seq", "tp", None), P(), P(None, "seq", None, "tp"), P(), P())
    out_specs = P("seq", None, "tp")
    return jax.shard_map(shards, mesh=mesh, in_specs=in_specs, out_specs=out_specs, check_vma=False)
```

profile of v0, /device:TPU:0, one launch (start us, length us, event | category | flops | bytes accessed | tf_op | source)
XLA Modules:
  0.0 245.8 jit_solution(11908729326327662818)
XLA Ops:
  0.0 6.8 %copy.57 = bf16[2,1,256,3072]{3,0,1,2:T(2,128)(2,1)} copy(bf16[2,1,256,3072]{3,2,1,0:T(8,128)(2,1)} %param.5) | data formatting | bytes 6291456 | tf_op args[0]
  6.8 0.0 copy-start.4
  6.8 0.0 copy-start.5
  6.8 7.5 %all-to-all-start = ((bf16[2,1,256,3072]{3,0,1,2:T(2,128)(2,1)}), bf16[2,1,256,3072]{3,0,1,2:T(2,128)(2,1)S(1)}, u32[]{:S(2)}, u32[]{:S(2)}) async-start(bf16[2,1,256,3072]{3,0,1,2:T(2,128)(2,1)} %copy.57), calls=%async_computation | async-start | bytes 6291456 | tf_op jit(solution)/shard_map/all_to_all | solution.py:77
  14.3 0.0 copy-done.4
  14.3 0.0 copy-done.5
  14.3 0.1 select_reduce_fusion
  14.5 0.7 gather_fusion
  15.2 58.5 %all-to-all-done = bf16[2,1,256,3072]{3,0,1,2:T(2,128)(2,1)S(1)} async-done(((bf16[2,1,256,3072]{3,0,1,2:T(2,128)(2,1)}), bf16[2,1,256,3072]{3,0,1,2:T(2,128)(2,1)S(1)}, u32[]{:S(2)}, u32[]{:S(2)}) %all-to-all-start) | async-done | bytes 3145760 | tf_op jit(solution)/shard_map/all_to_all | solution.py:77
  73.7 2.4 copy.58
  76.1 2.6 %gather_fusion.1 = bf16[16,2,16,3072]{3,2,1,0:T(8,128)(2,1)S(1)} fusion(bf16[2,16,16,3072]{3,2,1,0:T(8,128)(2,1)} %bitcast.89, s32[1024]{0:T(1024)S(1)} %pad_clamp_fusion), kind=kCustom, calls=%fused_computation.1 | custom fusion | bytes 6291520 | tf_op jit(solution)/shard_map/jit(_take)/gather | solution.py:78
  78.7 0.4 select_bitcast_fusion
  79.1 85.0 %all_to_all.39 = bf16[2,16,16,3072]{3,2,0,1:T(8,128)(2,1)S(1)} all-to-all(bf16[2,16,16,3072]{3,2,0,1:T(8,128)(2,1)S(1)} %select_bitcast_fusion), channel_id=1, replica_groups=mesh['seq'=16,'tp'=2] {'seq'}, dimensions={1} | all-to-all | bytes 6291456 | tf_op jit(solution)/shard_map/all_to_all | solution.py:80
  164.1 0.2 copy.59
  164.4 5.7 %copy.60 = bf16[2,1,256,3072]{2,0,1,3:T(2,128)(2,1)} copy(bf16[2,1,256,3072]{3,2,0,1:T(8,128)(2,1)S(1)} %bitcast.90) | data formatting | bytes 6291456 | tf_op jit(solution)/shard_map/all_to_all | solution.py:80
  170.1 0.0 copy-start.6
  170.1 4.1 %all-to-all-start.2 = ((bf16[2,1,256,3072]{2,0,1,3:T(2,128)(2,1)}), bf16[2,1,256,3072]{2,0,1,3:T(2,128)(2,1)S(1)}, u32[]{:S(2)}, u32[]{:S(2)}) async-start(bf16[2,1,256,3072]{2,0,1,3:T(2,128)(2,1)} %copy.60), calls=%async_computation.2 | async-start | bytes 6291456 | tf_op jit(solution)/shard_map/all_to_all | solution.py:79
  174.2 0.6 dynamic-slice.4
  175.4 0.0 copy-done.6
  175.4 0.6 dynamic-slice.5
  176.0 3.1 %fusion.23 = (bf16[1,1,256,1536]{3,2,1,0:T(8,128)(2,1)}, bf16[1,1,256,1536]{3,2,1,0:T(8,128)(2,1)}, bf16[1,1,256,1536]{3,2,1,0:T(8,128)(2,1)}) fusion(bf16[3,1,256,1536]{3,2,1,0:T(8,128)(2,1)} %param.7), kind=kLoop, calls=%fused_computation.48 | loop fusion | bytes 4718592 | tf_op jit(solution)/shard_map/slice | solution.py:66
  179.1 2.3 copy.63
  181.4 2.3 copy.67
  183.7 2.3 copy.64
  186.7 2.2 fusion.2
  188.9 0.0 copy-start
  188.9 1.9 copy-done
  190.9 0.9 convert_reduce_fusion.1
  191.7 19.7 %all-to-all-done.2 = bf16[2,1,256,3072]{2,0,1,3:T(2,128)(2,1)S(1)} async-done(((bf16[2,1,256,3072]{2,0,1,3:T(2,128)(2,1)}), bf16[2,1,256,3072]{2,0,1,3:T(2,128)(2,1)S(1)}, u32[]{:S(2)}, u32[]{:S(2)}) %all-to-all-start.2) | async-done | bytes 3145760 | tf_op jit(solution)/shard_map/all_to_all | solution.py:79
  211.4 0.4 copy.61
  211.8 1.4 fusion.22
  213.2 10.7 %copy.65 = bf16[1,1,2,256,1536]{3,2,4,1,0:T(2,128)(2,1)} copy(bf16[1,1,2,256,1536]{3,4,2,0,1:T(8,128)(2,1)S(1)} %get-tuple-element.86) | data formatting | bytes 3145728 | tf_op jit(solution)/shard_map/slice | solution.py:88
  223.9 2.8 %reshape_squeeze.18 = bf16[512,16,96]{0,2,1:T(8,128)(2,1)S(1)} reshape(bf16[1,1,2,256,1536]{3,2,4,1,0:T(2,128)(2,1)} %copy.65) | data formatting | bytes 3145728 | tf_op jit(solution)/shard_map/reshape;squeeze | solution.py:88
  226.7 0.0 copy-start.2
  226.7 4.9 %copy.62 = bf16[1,1,2,256,1536]{3,2,4,1,0:T(2,128)(2,1)} copy(bf16[1,1,2,256,1536]{3,4,2,0,1:T(8,128)(2,1)} %get-tuple-element.85) | data formatting | bytes 3145728 | tf_op jit(solution)/shard_map/slice | solution.py:87
  231.6 3.8 %reshape_squeeze.15 = bf16[512,16,96]{0,2,1:T(8,128)(2,1)} reshape(bf16[1,1,2,256,1536]{3,2,4,1,0:T(2,128)(2,1)} %copy.62) | data formatting | bytes 3145728 | tf_op jit(solution)/shard_map/reshape;squeeze | solution.py:87
  235.4 0.0 copy-done.2
  235.4 3.3 %bitcast_reduce_fusion = (f32[16,256]{1,0:T(8,128)S(1)}, f32[16,512,256]{2,1,0:T(8,128)S(1)}) fusion(pred[512]{0:T(512)(128)(4,1)S(1)} %iota_compare_fusion.2, bf16[512,16,96]{0,2,1:T(8,128)(2,1)} %reshape_squeeze.15, bf16[256,16,96]{0,2,1:T(8,128)(2,1)S(1)} %bitcast.92), kind=kOutput, calls=%fused_computation.3 | convolution fusion | flops 408940544 | bytes 10764800 | tf_op jit(solution)/shard_map/while/body/eval_jaxpr/qhd,khd->hqk/dot_general | solution.py:25
  238.7 2.1 convert_reduce_fusion
  240.9 0.0 copy-start.1
  240.9 0.0 copy-start.3
  240.9 0.8 fusion.24
  241.7 1.3 copy-done.1
  243.1 0.2 copy-done.3
  243.3 1.3 fusion.7
  244.6 1.2 copy.69
  (7 shorter events, 0.1 us)
Async XLA Ops:
  6.8 7.5 %copy-start.4 = (s32[16]{0:T(128)S(1)}, s32[16]{0:T(128)}, u32[]{:S(2)}) copy-start(s32[16]{0:T(128)} %param.8) | copy-start | bytes 196
  6.8 7.6 %copy-start.5 = (s32[16]{0:T(128)S(1)}, s32[16]{0:T(128)}, u32[]{:S(2)}) copy-start(s32[16]{0:T(128)} %param.9) | copy-start | bytes 196
  6.8 66.9 %all-to-all-start = ((bf16[2,1,256,3072]{3,0,1,2:T(2,128)(2,1)}), bf16[2,1,256,3072]{3,0,1,2:T(2,128)(2,1)S(1)}, u32[]{:S(2)}, u32[]{:S(2)}) async-start(bf16[2,1,256,3072]{3,0,1,2:T(2,128)(2,1)} %copy.57), calls=%async_computation | async-start | bytes 6291456 | tf_op jit(solution)/shard_map/all_to_all | solution.py:77
  170.1 5.3 %copy-start.6 = (s32[16]{0:T(128)S(1)}, s32[16]{0:T(128)}, u32[]{:S(2)}) copy-start(s32[16]{0:T(128)} %param.6) | copy-start | bytes 196
  170.1 41.3 %all-to-all-start.2 = ((bf16[2,1,256,3072]{2,0,1,3:T(2,128)(2,1)}), bf16[2,1,256,3072]{2,0,1,3:T(2,128)(2,1)S(1)}, u32[]{:S(2)}, u32[]{:S(2)}) async-start(bf16[2,1,256,3072]{2,0,1,3:T(2,128)(2,1)} %copy.60), calls=%async_computation.2 | async-start | bytes 6291456 | tf_op jit(solution)/shard_map/all_to_all | solution.py:79
  188.9 1.9 copy-start
  226.7 8.7 %copy-start.2 = (bf16[1,1,256,1536]{2,3,1,0:T(8,128)(2,1)S(1)}, bf16[1,1,256,1536]{2,3,1,0:T(8,128)(2,1)}, u32[]{:S(2)}) copy-start(bf16[1,1,256,1536]{2,3,1,0:T(8,128)(2,1)} %copy.63) | copy-start | bytes 2359300
  240.9 2.2 copy-start.1
  240.9 2.4 copy-start.3
where the time goes:
time: 247 us; the launch traced here: 246 us
  blocking collectives  85 us (34%)
  waiting for transfers between devices  78.2 us (32%)
  local copies, waits for them, and re-layouts  58.2 us (24%)
  starting transfers between devices  11.6 us (5%)
  matrix products  7.68 us (3%)
  other arithmetic  3.58 us (1%)
    all_to_all x1, blocking collectives, shards(): lax.all_to_all(ordered, 'seq', split_axis=1, concat_axis=2, tiled=True)  85 us
    all_to_all x1, waiting for transfers between devices, shards(): lax.all_to_all(cache, 'seq', split_axis=2, concat_axis=1, tiled=True)  58.5 us
    all_to_all x1, waiting for transfers between devices, shards(): lax.all_to_all(lax.all_to_all(ordered, 'seq', split_axis=1, concat_axis=2...  19.7 us
    slice x1, local copies, waits for them, and re-layouts, shards(): old_values = moved[1, 0].reshape(position_count, head_count, HD)  10.7 us
    unnamed x15, local copies, waits for them, and re-layouts  10.3 us
    all_to_all x1, starting transfers between devices, shards(): lax.all_to_all(cache, 'seq', split_axis=2, concat_axis=1, tiled=True)  7.52 us
    slice x2, local copies, waits for them, and re-layouts, shards(): old_keys = moved[0, 0].reshape(position_count, head_count, HD)  6.32 us
    all_to_all x2, local copies, waits for them, and re-layouts, shards(): lax.all_to_all(ordered, 'seq', split_axis=1, concat_axis=2, tiled=True)  5.92 us
  transfers between devices with their start and end apart: 2, of which 2 were waited for; matrix products, arithmetic and copies ran while one was open for 6% of the time, Pallas kernels for 0%

commit v1 on v0

--- a/solution.py
+++ b/solution.py
@@ -1,11 +1,287 @@
+import functools
 import math
 
 import jax
 import jax.numpy as jnp
 from jax import lax
+from jax.experimental import pallas as pl
+from jax.experimental.pallas import tpu as pltpu
 from jax.sharding import PartitionSpec as P
 
 HD = 96
+QUAD = 4 * HD
+LANES = 128
+MESH = pl.DeviceIdType.MESH
+FACTOR = 1.0 / math.sqrt(HD)
+WINDOWS = ((0, 128, 0), (0, 256, 96), (128, 256, 64), (256, 128, 32))
+
+
+def attend(queries, key_rows, value_rows, keep, first_lane):
+    width = queries.shape[1]
+    lane = lax.broadcasted_iota(jnp.int32, (1, width), 1)
+    mine = jnp.where((lane >= first_lane) & (lane < first_lane + HD), 1.0, 0.0)
+    mask = mine.astype(jnp.bfloat16)
+    rest = (1.0 - mine).astype(jnp.bfloat16)
+    scores = lax.dot_general(
+        queries * mask, key_rows, (((1,), (1,)), ((), ())), preferred_element_type=jnp.float32
+    )
+    scores = jnp.where(keep, scores, -jnp.inf)
+    top = jnp.max(scores, axis=1, keepdims=True)
+    weights = jnp.exp((scores - top) * FACTOR).astype(jnp.bfloat16)
+    mixed = jnp.dot(weights, value_rows * mask + rest, preferred_element_type=jnp.float32)
+    free = 0 if first_lane > 0 else HD
+    total = mixed[:, free : free + 1]
+    return mixed * (1.0 / total), top * FACTOR + jnp.log(total)
+
+
+def attend_quad(load_queries, load_keys, load_values, keep):
+    parts, logs = [], []
+    for start, width, first_lane in WINDOWS:
+        mix, log = attend(
+            load_queries(start, width), load_keys(start, width), load_values(start, width), keep, first_lane
+        )
+        parts.append(mix)
+        logs.append(log)
+    lane = lax.broadcasted_iota(jnp.int32, (1, LANES), 1)
+    tiles = (
+        jnp.where(lane < 96, parts[0], parts[1][:, :LANES]),
+        jnp.where(lane < 64, parts[1][:, LANES:], parts[2][:, :LANES]),
+        jnp.where(lane < 32, parts[2][:, LANES:], parts[3]),
+    )
+    return tiles, logs
+
+
+def kernel(
+    n, tps, quads, source_ref, slot_ref, length_ref, cache_ref, group_ref, out_ref,
+    kv, own, own_mix, own_log, old_log, *rest,
+):
+    spread, staged, asked, partial, landed, restaged, answer = (
+        rest[i * quads : (i + 1) * quads] for i in range(7)
+    )
+    send_sem, recv_sem, kv_send, kv_recv, local_sem = rest[7 * quads :]
+    me, tp = lax.axis_index("seq"), lax.axis_index("tp")
+    rows = group_ref.shape[2]
+    block = rows // n
+    width = group_ref.shape[3]
+    heads = width // HD
+    positions = cache_ref.shape[2]
+    my_rows = pl.ds(pl.multiple_of(me * block, block), block)
+
+    barrier = pltpu.get_barrier_semaphore()
+
+    @pl.loop(1, n)
+    def _(k):
+        pl.semaphore_signal(barrier, inc=1, device_id={"seq": lax.rem(me + k, n)}, device_id_type=MESH)
+
+    @pl.loop(1, tps)
+    def _(k):
+        pl.semaphore_signal(barrier, inc=1, device_id={"tp": lax.rem(tp + k, tps)}, device_id_type=MESH)
+
+    pl.semaphore_wait(barrier, n + tps - 2)
+
+    def send(phase, g, src, dst, to):
+        pltpu.make_async_remote_copy(
+            src_ref=src, dst_ref=dst, send_sem=send_sem.at[phase, g], recv_sem=recv_sem.at[phase, g],
+            device_id={"seq": to}, device_id_type=MESH,
+        ).start()
+
+    def wait(sem, phase, g, buffer):
+        some = buffer.at[pl.ds(0, n - 1)]
+        pltpu.make_async_copy(some, some, sem.at[phase, g]).wait()
+
+    def wait_rows(sem, phase, g, buffer):
+        some = buffer.at[pl.ds(0, (n - 1) * block)]
+        pltpu.make_async_copy(some, some, sem.at[phase, g]).wait()
+
+    local = {}
+    for g in range(quads):
+        columns = pl.ds(g * QUAD, QUAD)
+        local[g] = (
+            pltpu.make_async_copy(group_ref.at[0, 0, my_rows, columns], spread[g].at[me], local_sem.at[0, g]),
+            pltpu.make_async_copy(group_ref.at[:, 0, :, columns], own.at[g], local_sem.at[1, g]),
+            pltpu.make_async_copy(
+                cache_ref.at[:, 0, :, pl.ds(pl.multiple_of(tp * width + g * QUAD, LANES), QUAD)],
+                kv.at[g, :, pl.ds(pl.multiple_of(tp * positions, positions), positions)],
+                local_sem.at[2, g],
+            ),
+        )
+
+        @pl.loop(1, n)
+        def _(k):
+            to = lax.rem(me + k, n)
+            send(
+                0, g, group_ref.at[0, 0, pl.ds(pl.multiple_of(to * block, block), block), columns],
+                spread[g].at[me], to,
+            )
+
+        local[g][0].start()
+
+        @pl.loop(1, tps)
+        def _(k):
+            to = lax.rem(tp + k, tps)
+            pltpu.make_async_remote_copy(
+                src_ref=cache_ref.at[:, 0, :, pl.ds(pl.multiple_of(to * width + g * QUAD, LANES), QUAD)],
+                dst_ref=kv.at[g, :, pl.ds(pl.multiple_of(tp * positions, positions), positions)],
+                send_sem=kv_send.at[g], recv_sem=kv_recv.at[g], device_id={"tp": to}, device_id_type=MESH,
+            ).start()
+
+        local[g][1].start()
+        local[g][2].start()
+
+    lane = lax.broadcasted_iota(jnp.int32, (1, LANES), 1)
+    causal = lax.broadcasted_iota(jnp.int32, (rows, rows), 0) >= lax.broadcasted_iota(jnp.int32, (rows, rows), 1)
+
+    own_log[...] = jnp.zeros_like(own_log)
+    for g in range(quads):
+        wait(recv_sem, 0, g, spread[g])
+        local[g][0].wait()
+
+        asked[g][my_rows, :] = spread[g][source_ref[me]]
+
+        @pl.loop(1, n)
+        def _(k):
+            to = lax.rem(me + k, n)
+            staged[g][to] = spread[g][source_ref[to]]
+            send(1, g, staged[g].at[to], asked[g].at[my_rows], to)
+
+        local[g][1].wait()
+        tiles, logs = attend_quad(
+            lambda s, w: own[g, 0, :, s : s + w],
+            lambda s, w: own[g, 1, :, s : s + w],
+            lambda s, w: own[g, 2, :, s : s + w],
+            causal,
+        )
+        for i, tile in enumerate(tiles):
+            own_mix[:, g * QUAD + i * LANES : g * QUAD + (i + 1) * LANES] = tile
+        for i, log in enumerate(logs):
+            own_log[...] = jnp.where(lane == g * 4 + i, log, own_log[...])
+
+    live = lax.broadcasted_iota(jnp.int32, (1, tps * positions), 1) < length_ref[0]
+    old_log[...] = jnp.zeros_like(old_log)
+    for g in range(quads):
+        wait_rows(recv_sem, 1, g, asked[g])
+        local[g][2].wait()
+        arrived = kv.at[g, :, pl.ds(0, (tps - 1) * positions)]
+        pltpu.make_async_copy(arrived, arrived, kv_recv.at[g]).wait()
+        tiles, logs = attend_quad(
+            lambda s, w: asked[g][:, s : s + w],
+            lambda s, w: kv[g, 0, :, s : s + w],
+            lambda s, w: kv[g, 1, :, s : s + w],
+            live,
+        )
+        for i, tile in enumerate(tiles):
+            partial[g][:, i * LANES : (i + 1) * LANES] = tile.astype(jnp.bfloat16)
+        for i, log in enumerate(logs):
+            old_log[...] = jnp.where(lax.rem(lane, heads) == g * 4 + i, log, old_log[...])
+        if g == quads - 1:
+            log = old_log[...]
+            high = log.astype(jnp.bfloat16).astype(jnp.float32)
+            middle = (log - high).astype(jnp.bfloat16).astype(jnp.float32)
+            low = log - high - middle
+            pieces = jnp.where(lane < heads, high, jnp.where(lane < 2 * heads, middle, low))
+            partial[g][:, QUAD:] = pieces.astype(jnp.bfloat16)
+
+        landed[g][me] = partial[g][my_rows, :]
+
+        @pl.loop(1, n)
+        def _(k):
+            to = lax.rem(me + k, n)
+            send(
+                2, g, partial[g].at[pl.ds(pl.multiple_of(to * block, block), block)], landed[g].at[me], to
+            )
+
+    for g in range(quads):
+        wait(recv_sem, 2, g, landed[g])
+        answer[g][my_rows, :] = landed[g][slot_ref[me]]
+
+        @pl.loop(1, n)
+        def _(k):
+            to = lax.rem(me + k, n)
+            restaged[g][to] = landed[g][slot_ref[to]]
+            send(3, g, restaged[g].at[to], answer[g].at[my_rows], to)
+
+    for g in range(quads):
+        wait_rows(recv_sem, 3, g, answer[g])
+    pieces = answer[quads - 1][:, QUAD:].astype(jnp.float32)
+    log = pieces + pltpu.roll(pieces, LANES - heads, 1) + pltpu.roll(pieces, LANES - 2 * heads, 1)
+    share = 1.0 / (1.0 + jnp.exp(own_log[...] - log))
+    for g in range(quads):
+        parts = [share[:, g * 4 + i : g * 4 + i + 1] for i in range(4)]
+        for i, (edge, left, right) in enumerate(((96, 0, 1), (64, 1, 2), (32, 2, 3))):
+            portion = jnp.where(lane < edge, parts[left], parts[right])
+            columns = slice(g * QUAD + i * LANES, g * QUAD + (i + 1) * LANES)
+            mine = own_mix[:, columns]
+            theirs = answer[g][:, i * LANES : (i + 1) * LANES].astype(jnp.float32)
+            out_ref[0, :, columns] = (mine + portion * (theirs - mine)).astype(jnp.bfloat16)
+
+    for g in range(quads):
+        wait(send_sem, 0, g, spread[g])
+        wait(send_sem, 1, g, staged[g])
+        wait(send_sem, 2, g, landed[g])
+        wait(send_sem, 3, g, restaged[g])
+        sent = kv.at[g, :, pl.ds(0, (tps - 1) * positions)]
+        pltpu.make_async_copy(sent, sent, kv_send.at[g]).wait()
+
+
+def fused(n, tps, cache, cache_len, group, group_req, req_order):
+    slot_of = inverse_table(req_order)
+    index_of = inverse_table(group_req)
+    slot_for_index = small_take(slot_of, group_req)
+    index_for_slot = small_take(index_of, req_order)
+    my_request = small_take(req_order, lax.axis_index("seq")[None])
+    length = small_take(cache_len, my_request)
+    rows, width = group.shape[2], group.shape[3]
+    positions = cache.shape[2]
+    quads = width // QUAD
+    block = rows // n
+    widths = [QUAD] * (quads - 1) + [QUAD + LANES]
+
+    def blocks(sizes):
+        return [pltpu.VMEM((n, block, w), jnp.bfloat16) for w in sizes]
+
+    def whole(sizes):
+        return [pltpu.VMEM((rows, w), jnp.bfloat16) for w in sizes]
+
+    plain = [QUAD] * quads
+    return pl.pallas_call(
+        functools.partial(kernel, n, tps, quads),
+        out_shape=jax.ShapeDtypeStruct((1, rows, width), jnp.bfloat16),
+        in_specs=[pl.BlockSpec(memory_space=pltpu.SMEM)] * 3 + [pl.BlockSpec(memory_space=pl.ANY)] * 2,
+        out_specs=pl.BlockSpec(memory_space=pltpu.VMEM),
+        scratch_shapes=[
+            pltpu.VMEM((quads, 2, tps * positions, QUAD), jnp.bfloat16),
+            pltpu.VMEM((quads, 3, rows, QUAD), jnp.bfloat16),
+            pltpu.VMEM((rows, width), jnp.float32),
+            pltpu.VMEM((rows, LANES), jnp.float32),
+            pltpu.VMEM((rows, LANES), jnp.float32),
+            *blocks(plain), *blocks(plain), *whole(plain), *whole(widths),
+            *blocks(widths), *blocks(widths), *whole(widths),
+            pltpu.SemaphoreType.DMA((4, quads)),
+            pltpu.SemaphoreType.DMA((4, quads)),
+            pltpu.SemaphoreType.DMA((quads,)),
+            pltpu.SemaphoreType.DMA((quads,)),
+            pltpu.SemaphoreType.DMA((3, quads)),
+        ],
+        compiler_params=pltpu.CompilerParams(
+            collective_id=0, has_side_effects=True, vmem_limit_bytes=48 * 2**20
+        ),
+        cost_estimate=pl.CostEstimate(
+            flops=4 * rows * width * (rows + tps * positions),
+            bytes_accessed=cache.size * 2 + group.size * 2,
+            transcendentals=rows * (rows + tps * positions) * width // HD,
+        ),
+    )(index_for_slot, slot_for_index, length, cache, group)
+
+
+def small_take(table, index):
+    hits = index[:, None] == jnp.arange(table.shape[0], dtype=jnp.int32)[None, :]
+    return jnp.sum(jnp.where(hits, table[None, :], 0), axis=1)
+
+
+def pick(array, index):
+    return jnp.stack(
+        [lax.dynamic_index_in_dim(array, index[i], 1, keepdims=False) for i in range(array.shape[1])], axis=1
+    )
 
 
 def inverse_table(permutation):
@@ -75,7 +351,7 @@
         queries, new_keys, new_values, causal_rows, group_block, row_count // group_block, factor
     )
     spread = lax.all_to_all(cache, "seq", split_axis=2, concat_axis=1, tiled=True)
-    ordered = jnp.take(spread, source_slot, axis=1)
+    ordered = pick(spread, source_slot)
     moved = lax.all_to_all(
         lax.all_to_all(ordered, "seq", split_axis=1, concat_axis=2, tiled=True),
         "tp",
@@ -101,6 +377,15 @@
 
 
 def solution(mesh):
+    n, tps = mesh.shape["seq"], mesh.shape["tp"]
+
+    def run(cache, cache_len, group, group_req, req_order):
+        rows, width = group.shape[2], group.shape[3]
+        whole_blocks = rows % (16 * n) == 0 and width % QUAD == 0 and 3 * (width // HD) <= LANES
+        if whole_blocks and tps > 1 and cache.shape[2] % 16 == 0:
+            return fused(n, tps, cache, cache_len, group, group_req, req_order)
+        return shards(cache, cache_len, group, group_req, req_order)
+
     in_specs = (P(None, "seq", "tp", None), P(), P(None, "seq", None, "tp"), P(), P())
     out_specs = P("seq", None, "tp")
-    return jax.shard_map(shards, mesh=mesh, in_specs=in_specs, out_specs=out_specs, check_vma=False)
+    return jax.shard_map(run, mesh=mesh, in_specs=in_specs, out_specs=out_specs, check_vma=False)

time: 247 us -> 87.8 us (0.36)
  blocking collectives: 85 us -> 0 us
  Pallas kernels: 0 us -> 79.2 us
  waiting for transfers between devices: 78.2 us -> 0 us
  local copies, waits for them, and re-layouts: 58.2 us -> 2.55 us
  starting transfers between devices: 11.6 us -> 0 us
  matrix products: 7.68 us -> 0 us
    all_to_all x1 -> x0, blocking collectives: 85 us -> none  [shards(): lax.all_to_all(ordered, 'seq', split_axis=1, concat_axis=2, tiled=True)]
    pallas_call x0 -> x1, Pallas kernels: none -> 79.2 us  [fused(): pl.pallas_call(functools.partial(kernel, n, tps, quads), out_shape=jax.Sh...]
    all_to_all x2 -> x0, waiting for transfers between devices: 78.2 us -> none  [the longest x1 58.5 us: shards(): lax.all_to_all(cache, 'seq', split_axis=2, concat_axis=1, tiled=True)]
    slice x7 -> x0, local copies, waits for them, and re-layouts: 27 us -> none  [the longest x1 10.7 us: shards(): old_values = moved[1, 0].reshape(position_count, head_count, HD)]
    all_to_all x2 -> x0, starting transfers between devices: 11.6 us -> none  [the longest x1 7.52 us: shards(): lax.all_to_all(cache, 'seq', split_axis=2, concat_axis=1, tiled=True)]
    all_to_all x4 -> x0, local copies, waits for them, and re-layouts: 8.76 us -> none  [the longest x2 5.92 us: shards(): lax.all_to_all(ordered, 'seq', split_axis=1, concat_axis=2, tiled=True)]
    another operation x4 -> x0, local copies, waits for them, and re-layouts: 7.75 us -> none  [the longest x1 3.76 us: shards(): old_keys = moved[0, 0].reshape(position_count, head_count, HD)]
    unnamed x15 -> x3, local copies, waits for them, and re-layouts: 10.3 us -> 2.55 us
  transfers between devices with their start and end apart: 2 -> 0, of which waited for: 2 -> 0; matrix products, arithmetic and copies ran while one was open for 6% -> 0% of each run, Pallas kernels for 0% -> 0%
where the time goes in v1:
time: 87.8 us; the launch traced here: 87.6 us
  Pallas kernels  79.2 us (90%)
  other arithmetic  5.83 us (7%)
  local copies, waits for them, and re-layouts  2.55 us (3%)
    pallas_call x1, Pallas kernels, fused(): pl.pallas_call(functools.partial(kernel, n, tps, quads), out_shape=jax.Sh...  79.2 us
    reduce_sum x4, other arithmetic, small_take(): return jnp.sum(jnp.where(hits, table[None, :], 0), axis=1)  5.06 us
    unnamed x3, local copies, waits for them, and re-layouts  2.55 us

profile of v1, /device:TPU:0, one launch (start us, length us, event | category | flops | bytes accessed | tf_op | source)
XLA Modules:
  0.0 87.6 jit_solution(8861572138807506906)
XLA Ops:
  0.0 1.3 %fusion = s32[]{:T(128)} fusion(s32[16]{0:T(128)} %param.9, s32[]{:T(128)S(6)} %axis_index.15), kind=kLoop, calls=%fused_computation.10 | loop fusion | flops 47 | bytes 72 | tf_op jit(solution)/shard_map/reduce_sum | solution.py:278
  1.3 2.0 %fusion.1 = s32[]{:T(128)} fusion(s32[16]{0:T(128)} %param.6, s32[]{:T(128)} %fusion), kind=kLoop, calls=%fused_computation.11 | loop fusion | flops 47 | bytes 72 | tf_op jit(solution)/shard_map/reduce_sum | solution.py:278
  3.3 0.8 select_reduce_fusion.1
  4.1 0.9 %select_reduce_fusion = (s32[16]{0:T(128)S(1)}, s32[16]{0:T(128)S(1)}) fusion(s32[16]{0:T(128)S(1)} %select_reduce_fusion.1, s32[16]{0:T(128)} %param.8), kind=kLoop, calls=%fused_computation | loop fusion | flops 1504 | bytes 256 | tf_op jit(solution)/shard_map/reduce_sum | solution.py:278
  5.0 0.8 select_reduce_fusion.2.source_ref
  5.8 0.0 copy-start
  5.8 1.7 %copy-done = bf16[3,1,256,1536]{3,2,1,0:T(8,128)(2,1)S(1)} copy-done((bf16[3,1,256,1536]{3,2,1,0:T(8,128)(2,1)S(1)}, bf16[3,1,256,1536]{3,2,1,0:T(8,128)(2,1)}, u32[]{:S(2)}) %copy-start) | copy-done | bytes 2359320
  7.5 79.2 %shard_map.55 = bf16[1,256,1536]{2,1,0:T(8,128)(2,1)S(1)} custom-call(s32[16]{0:T(128)S(1)} %select_reduce_fusion.2.source_ref, s32[16]{0:T(128)S(1)} %get-tuple-element.5.slot_ref, s32[1]{0:T(128)} %bitcast.length_ref, bf16[2,1,256,3072]{3,2,1,0:T(8,128)(2,1)} %cache_ref.1, bf16[3,1,256,1536]{3,2,1,0:T(8,128)(2,1)S(1)} %copy-done), custom_call_target="tpu_custom_call" | custom-call | flops 1207959552 | bytes 5505024 | tf_op jit(solution)/shard_map/pallas_call | solution.py:246
  86.8 0.9 %copy.7 = bf16[1,256,1536]{2,1,0:T(8,128)(2,1)} copy(bf16[1,256,1536]{2,1,0:T(8,128)(2,1)S(1)} %shard_map.55) | data formatting | bytes 1572864
Async XLA Ops:
  5.8 1.7 %copy-start = (bf16[3,1,256,1536]{3,2,1,0:T(8,128)(2,1)S(1)}, bf16[3,1,256,1536]{3,2,1,0:T(8,128)(2,1)}, u32[]{:S(2)}) copy-start(bf16[3,1,256,1536]{3,2,1,0:T(8,128)(2,1)} %group_ref.1) | copy-start | bytes 7077892
